TPU v7x, 128 devices: a whole 4x4x4 slice. The times are simulated.
128 devices in a mesh: shot: 16 (over z, x), rcv: 8 (over y, core).
Axes of the slice: x: 4, y: 4, z: 4, core: 2. Of those that a mesh axis runs over, the one named last changes fastest.
Arguments:
- traces: bfloat16 [512, 512, 1024], P('shot', 'rcv'), may hold values from -6 to 6
- aperture_lists: int32 [16, 8, 8], P('shot', 'rcv'), may hold values from 0 to 15, as said below
- aperture_counts: int32 [16, 8], P('shot', 'rcv'), may hold values from 4 to 8
Outputs:
- multiples: float32 [64, 2, 512, 512], P(None, None, 'shot', 'rcv')
Inputs may be any that keep to these rules, and one draw needn't show every extreme that they name: `aperture_lists`: for tile (i, j), entries 0 to aperture_counts[i, j] - 1 are consecutive rising x-block numbers (block b covers positions b * 32 to (b + 1) * 32 - 1) near the midpoint of the tile's shots and receivers; the other entries are 0.
All inputs are finite; a program needn't handle non-finite values.
Results may differ from a plain program's by a relative error of at most 0.0052.
Values may be sent and summed in bfloat16 or wider, within the bound.
A program may use at most 128 MiB of HBM per device.

v0:
```python
import math

import jax
import jax.numpy as jnp
from jax import lax
from jax.sharding import PartitionSpec as P

SHOTS_PER_INDEX = 32
NT = 1024
BAND = 32
APB = 8
FIRST = 32
SECOND = 128
FREQS = 64


def dft_table():
    sample = jnp.arange(NT, dtype=jnp.int32)
    freq_bins = jnp.concatenate(
        [FIRST + jnp.arange(BAND, dtype=jnp.int32), SECOND + jnp.arange(BAND, dtype=jnp.int32)]
    )
    phase = (sample[:, None] * freq_bins[None, :] % NT).astype(jnp.float32) * (2.0 * math.pi / NT)
    factor = 1.0 / math.sqrt(NT)
    return (jnp.concatenate([jnp.cos(phase), -jnp.sin(phase)], axis=1) * factor).astype(
        jnp.bfloat16
    )


def spectra(traces):
    shots, receivers, samples = traces.shape
    flat = jnp.dot(
        traces.reshape(shots * receivers, samples), dft_table(), preferred_element_type=jnp.float32
    )
    flat = flat.astype(jnp.bfloat16)
    return flat.reshape(shots, receivers, 2, FREQS).transpose(3, 2, 0, 1)


def complex_product(left, right):

    def mult(leading_operand, trailing_operand):
        return jnp.einsum(
            "ylp,ypi->yli", leading_operand, trailing_operand, preferred_element_type=jnp.float32
        )

    real_out = mult(left[:, 0], right[:, 0]) - mult(left[:, 1], right[:, 1])
    imag_out = mult(left[:, 0], right[:, 1]) + mult(left[:, 1], right[:, 0])
    return jnp.stack([real_out, imag_out], axis=1)


def local(traces, aperture_lists, aperture_counts):
    trace_spectrum = spectra(traces)
    block_list = aperture_lists[0, 0]
    live_count = aperture_counts[0, 0]
    slots = jnp.arange(APB, dtype=jnp.int32)
    live = slots < live_count
    shot_rows = lax.all_gather(trace_spectrum, "rcv", axis=3, tiled=True)
    columns = lax.all_gather(trace_spectrum, "shot", axis=2, tiled=True)
    blocks = jnp.arange(shot_rows.shape[3], dtype=jnp.int32) // SHOTS_PER_INDEX
    hits = live[None, :] & (block_list[None, :] == blocks[:, None])
    weights = jnp.any(hits, axis=1).astype(jnp.bfloat16)
    total = complex_product(shot_rows * weights, columns)
    return total * (1.0 / math.sqrt(APB * SHOTS_PER_INDEX))


def solution(mesh):
    placed = (P("shot", "rcv", None), P("shot", "rcv", None), P("shot", "rcv"))
    return jax.shard_map(
        local, mesh=mesh, in_specs=placed, out_specs=P(None, None, "shot", "rcv"), check_vma=False
    )
```

profile of v0, /device:TPU:0, one launch (start us, length us, event | category | flops | bytes accessed | tf_op | source)
XLA Modules:
  0.0 237.4 jit_solution(1368056321377087646)
XLA Ops:
  6.5 0.0 all-gather.3.cloned.1.call-start
  6.5 0.1 pad_add_fusion
  6.6 2.1 fusion.30
  8.7 4.0 %fusion.8 = bf16[2048,128]{0,1:T(8,128)(2,1)S(1)} fusion(bf16[2048,1024]{1,0:T(8,128)(2,1)} %bitcast.50, f32[1024,64]{1,0:T(8,128)S(1)} %get-tuple-element.8, f32[1024,64]{1,0:T(8,128)S(1)} %get-tuple-element.7), kind=kOutput, calls=%fused_computation.9 | convolution fusion | flops 537526272 | bytes 5242880 | tf_op jit(solution)/shard_map/dot_general | solution.py:31
  12.7 0.0 copy-start.3
  12.7 1.1 reshape.29
  13.8 2.9 %copy.20 = bf16[32,64,2,64]{3,0,2,1:T(8,128)(2,1)} copy(bf16[32,64,2,64]{1,0,3,2:T(8,128)(2,1)S(1)} %reshape.29) | data formatting | bytes 1048576 | tf_op jit(solution)/shard_map/reshape | solution.py:35
  16.7 0.0 all-gather.3.cloned.1.call-update
  16.7 0.2 all-gather.5.cloned.1.call-start
  16.9 1.4 copy.22
  18.3 0.0 all-gather.5.cloned.1.call-update
  19.0 0.0 copy-done.3
  19.0 0.1 and_reduce_fusion
  19.1 49.9 %all-gather.3.cloned.1.call-done = bf16[64,2,32,512]{0,2,1,3:T(8,128)(2,1)} async-done(((bf16[64,2,32,64]{0,2,1,3:T(8,128)(2,1)}), bf16[64,2,32,512]{0,2,1,3:T(8,128)(2,1)}) %all-gather.3.cloned.1.call-update) | async-done | bytes 4194320 | tf_op jit(solution)/shard_map/all_gather | solution.py:56
  69.1 12.0 %copy.21 = bf16[64,2,32,512]{3,2,0,1:T(8,128)(2,1)} copy(bf16[64,2,32,512]{0,2,1,3:T(8,128)(2,1)} %all-gather.3.cloned.1.call-done) | data formatting | bytes 8388608 | tf_op jit(solution)/shard_map/all_gather | solution.py:56
  81.1 4.9 %broadcast_multiply_fusion = bf16[64,2,32,512]{3,2,0,1:T(8,128)(2,1)} fusion(bf16[64,2,32,512]{3,2,0,1:T(8,128)(2,1)} %copy.21, bf16[512]{0:T(512)(128)(2,1)S(1)} %convert_element_type.23), kind=kLoop, calls=%fused_computation.13 | loop fusion | flops 2097152 | bytes 8389632 | tf_op jit(solution)/shard_map/mul | solution.py:61
  86.0 96.9 %all-gather.5.cloned.1.call-done = bf16[64,2,512,64]{3,0,1,2:T(8,128)(2,1)} async-done(((bf16[64,2,32,64]{3,0,1,2:T(8,128)(2,1)}), bf16[64,2,512,64]{3,0,1,2:T(8,128)(2,1)}) %all-gather.5.cloned.1.call-update) | async-done | bytes 8388624 | tf_op jit(solution)/shard_map/all_gather | solution.py:57
  182.9 12.8 %fusion.36 = (bf16[64,1,512,64]{3,0,1,2:T(8,128)(2,1)}, bf16[64,1,512,64]{3,0,1,2:T(8,128)(2,1)}) fusion(bf16[64,2,512,64]{3,0,1,2:T(8,128)(2,1)} %all-gather.5.cloned.1.call-done), kind=kLoop, calls=%fused_computation.46 | loop fusion | bytes 16777216 | tf_op jit(solution)/shard_map/slice | solution.py:45
  195.6 9.7 %copy.28 = bf16[64,1,512,64]{2,3,0,1:T(8,128)(2,1)} copy(bf16[64,1,512,64]{3,0,1,2:T(8,128)(2,1)} %get-tuple-element.6) | data formatting | bytes 8388608
  205.4 0.0 copy-start
  205.4 4.2 %fusion = f32[64,32,64]{2,1,0:T(8,128)S(1)} fusion(bf16[64,1,512,64]{2,3,0,1:T(8,128)(2,1)} %copy.28, bf16[64,2,32,512]{3,2,0,1:T(8,128)(2,1)} %broadcast_multiply_fusion), kind=kOutput, calls=%fused_computation | convolution fusion | flops 134217728 | bytes 6815744 | tf_op jit(solution)/shard_map/ylp,ypi->yli/dot_general | solution.py:41
  209.5 0.0 copy-done
  209.5 2.8 %fusion.2 = f32[64,32,64]{2,1,0:T(8,128)S(1)} fusion(bf16[64,1,512,64]{2,3,0,1:T(8,128)(2,1)S(1)} %copy-done, bf16[64,2,32,512]{3,2,0,1:T(8,128)(2,1)} %broadcast_multiply_fusion), kind=kOutput, calls=%fused_computation.2 | convolution fusion | flops 134217728 | bytes 6815744 | tf_op jit(solution)/shard_map/ylp,ypi->yli/dot_general | solution.py:41
  212.4 9.8 %copy.27 = bf16[64,1,512,64]{2,3,0,1:T(8,128)(2,1)} copy(bf16[64,1,512,64]{3,0,1,2:T(8,128)(2,1)} %get-tuple-element.5) | data formatting | bytes 8388608
  222.1 0.0 copy-start.1
  222.1 0.0 copy-start.2
  222.1 4.2 %fusion.18 = f32[64,1,32,64]{3,2,0,1:T(8,128)S(1)} fusion(f32[64,32,64]{2,1,0:T(8,128)S(1)} %fusion, bf16[64,1,512,64]{2,3,0,1:T(8,128)(2,1)} %copy.27, bf16[64,2,32,512]{3,2,0,1:T(8,128)(2,1)} %broadcast_multiply_fusion), kind=kOutput, calls=%fused_computation.17 | convolution fusion | flops 134348800 | bytes 7340032 | tf_op jit(solution)/shard_map/ylp,ypi->yli/dot_general | solution.py:41
  226.3 0.0 copy-done.1
  226.3 1.1 copy-done.2
  227.4 1.2 fusion.12
  228.7 0.4 maximum_multiply_fusion
  229.1 1.5 copy.25
  (4 shorter events, 0.0 us)
Async XLA Ops:
  6.5 62.5 %all-gather.3.cloned.1.call-start = ((), (), s32[]{:S(2)}) async-start(), calls=%async_computation | async-start | bytes 9437184 | tf_op jit(solution)/shard_map/all_gather | solution.py:56
  12.7 6.3 %copy-start.3 = (s32[1,1,8]{2,1,0:T(1,128)S(1)}, s32[1,1,8]{2,1,0:T(1,128)}, u32[]{:S(2)}) copy-start(s32[1,1,8]{2,1,0:T(1,128)} %param.4) | copy-start | bytes 100
  16.7 166.2 %all-gather.5.cloned.1.call-start = ((), (), s32[]{:S(2)}) async-start(), calls=%async_computation.1 | async-start | bytes 17825792 | tf_op jit(solution)/shard_map/all_gather | solution.py:57
  205.4 4.2 %copy-start = (bf16[64,1,512,64]{2,3,0,1:T(8,128)(2,1)S(1)}, bf16[64,1,512,64]{2,3,0,1:T(8,128)(2,1)}, u32[]{:S(2)}) copy-start(bf16[64,1,512,64]{2,3,0,1:T(8,128)(2,1)} %copy.28) | copy-start | bytes 12582916
  222.1 4.2 %copy-start.1 = (bf16[64,1,512,64]{2,3,0,1:T(8,128)(2,1)S(1)}, bf16[64,1,512,64]{2,3,0,1:T(8,128)(2,1)}, u32[]{:S(2)}) copy-start(bf16[64,1,512,64]{2,3,0,1:T(8,128)(2,1)} %copy.27) | copy-start | bytes 12582916
  222.1 5.3 %copy-start.2 = (bf16[64,2,32,512]{3,2,0,1:T(8,128)(2,1)S(1)}, bf16[64,2,32,512]{3,2,0,1:T(8,128)(2,1)}, u32[]{:S(2)}) copy-start(bf16[64,2,32,512]{3,2,0,1:T(8,128)(2,1)} %broadcast_multiply_fusion) | copy-start | bytes 12582916
Sparse Core Ops, SparseCore 0:
  16.8 52.1 all-gather.2
  71.2 111.6 all-gather.4
where the time goes:
time: 239 us; the launch traced here: 237 us
  waiting for transfers between devices  147 us (62%)
  local copies, waits for them, and re-layouts  52.3 us (22%)
  matrix products  16.4 us (7%)
  between operations  14.1 us (6%)
  other arithmetic  7.52 us (3%)
    all_gather x1, waiting for transfers between devices, local(): columns = lax.all_gather(trace_spectrum, 'shot', axis=2, tiled=True)  96.9 us
    all_gather x1, waiting for transfers between devices, local(): shot_rows = lax.all_gather(trace_spectrum, 'rcv', axis=3, tiled=True)  49.9 us
    unnamed x10, local copies, waits for them, and re-layouts  20.6 us
    slice x1, local copies, waits for them, and re-layouts, complex_product(): real_out = mult(left[:, 0], right[:, 0]) - mult(left[:, 1], right[:, 1])  12.8 us
    dot_general x4, matrix products, mult(): jnp.einsum('ylp,ypi->yli', leading_operand, trailing_operand, preferred_e...  12.4 us
    all_gather x1, local copies, waits for them, and re-layouts, local(): shot_rows = lax.all_gather(trace_spectrum, 'rcv', axis=3, tiled=True)  12 us
    mul x1, other arithmetic, local(): total = complex_product(shot_rows * weights, columns)  4.88 us
  transfers between devices with their start and end apart: 2, of which 2 were waited for; matrix products, arithmetic and copies ran while one was open for 8% of the time, Pallas kernels for 0%

commit v1 on v0

v1 whole, which is shorter than its diff:
```python
import math

import jax
import jax.numpy as jnp
import ml_dtypes
import numpy as np
from jax import lax
from jax.experimental import pallas as pl
from jax.experimental.pallas import tpu as pltpu
from jax.sharding import PartitionSpec as P

MESH = pl.DeviceIdType.MESH

NT = 1024
BAND = 32
APB = 8
FIRST = 32
SECOND = 128
FREQS = 64
TS = 32
TR = 64
NS = 16
NY = 4
CHIPS = 64
SCALE = 1.0 / math.sqrt(APB * TS)
CHUNKS = 4


def dft_table():
    sample = np.arange(NT)
    bins = np.concatenate([FIRST + np.arange(BAND), SECOND + np.arange(BAND)])
    phase = (bins[:, None] * sample[None, :] % NT).astype(np.float32) * np.float32(2.0 * math.pi / NT)
    phase = phase.astype(np.float64)
    factor = 1.0 / math.sqrt(NT)
    return (np.concatenate([np.cos(phase), -np.sin(phase)], axis=0) * factor).astype(np.float32).astype(
        ml_dtypes.bfloat16
    )


def chip_of(shot, y, k):
    z = lax.rem(shot // 4 + k // 16, 4)
    x = lax.rem(lax.rem(shot, 4) + lax.rem(k // 4, 4), 4)
    return z * 4 + x, lax.rem(y + lax.rem(k, 4), 4)


def kernel(
    traces,
    table_hbm,
    lists,
    counts,
    out,
    tr,
    table,
    specf,
    spec,
    grid,
    mtab,
    mexp,
    masked,
    rhat,
    prod,
    back,
    load_sem,
    table_sem,
    send1,
    recv1,
    xsend,
    xrecv,
    send2,
    recv2,
    msend,
    mrecv,
):
    shot = lax.axis_index("shot")
    rcv = lax.axis_index("rcv")
    y = rcv // 2
    core = lax.rem(rcv, 2)
    z, x = shot // 4, lax.rem(shot, 4)
    me = y * NS + shot

    per = TS // CHUNKS
    pltpu.make_async_copy(table_hbm, table, table_sem).start()
    for n in range(CHUNKS):
        pltpu.make_async_copy(
            traces.at[pl.ds(n * per, per)], tr.at[pl.ds(n * per, per)], load_sem.at[n]
        ).start()

    barrier = pltpu.get_barrier_semaphore()
    pl.semaphore_signal(barrier, inc=1, device_id=(shot, y * 2 + 1 - core), device_id_type=MESH)

    def greet(k, carry):
        ts, ty = chip_of(shot, y, k)
        pl.semaphore_signal(barrier, inc=1, device_id=(ts, ty * 2 + core), device_id_type=MESH)
        return carry

    lax.fori_loop(1, CHIPS, greet, 0)

    lane = lax.broadcasted_iota(jnp.int32, (1, 128), 1)
    live = counts[0, 0]
    member = jnp.zeros((1, 128), jnp.float32)
    for k in range(APB):
        block = jnp.where(k < live, lists[0, k], -1)
        member = jnp.where(lane == block, 1.0, member)
    mtab[me] = member

    pl.semaphore_wait(barrier, CHIPS)

    def mask_copy(stage, d):
        if stage == 0:
            rows, to = pl.ds(me, 1), (z * 4 + lax.rem(x + d, 4), rcv)
        elif stage == 1:
            rows, to = pl.ds(y * NS + z * 4, 4), (lax.rem(z + d, 4) * 4 + x, rcv)
        else:
            rows, to = pl.ds(y * NS, NS), (shot, lax.rem(y + d, 4) * 2 + core)
        return pltpu.make_async_remote_copy(
            src_ref=mtab.at[rows],
            dst_ref=mtab.at[rows],
            send_sem=msend.at[stage * 3 + d - 1],
            recv_sem=mrecv.at[stage * 3 + d - 1],
            device_id=to,
            device_id_type=MESH,
        )

    def mask_start(stage):
        for d in (1, 2, 3):
            mask_copy(stage, d).start()

    def mask_wait(stage):
        for d in (1, 2, 3):
            mask_copy(stage, d).wait()

    mask_start(0)

    low = lax.broadcasted_iota(jnp.int32, (FREQS, 128), 1) < TR
    pltpu.make_async_copy(table_hbm, table, table_sem).wait()
    for n in range(CHUNKS):
        pltpu.make_async_copy(
            traces.at[pl.ds(n * per, per)], tr.at[pl.ds(n * per, per)], load_sem.at[n]
        ).wait()

        def transform(g, carry):
            first = n * per + g * 4
            rows = tr[pl.ds(first, 4)].reshape(4 * TR, NT)
            acc = lax.dot_general(
                table[...], rows, (((1,), (1,)), ((), ())), preferred_element_type=jnp.float32
            )
            for p in range(2):
                re = acc[:FREQS, p * 128 : p * 128 + 128]
                im = acc[FREQS:, p * 128 : p * 128 + 128]
                a = jnp.where(low, re, pltpu.roll(im, TR, 1))
                b = jnp.where(low, pltpu.roll(re, TR, 1), im)
                specf[pl.ds(first + 2 * p, FREQS, stride=TS), :] = a
                specf[pl.ds(first + 2 * p + 1, FREQS, stride=TS), :] = b
            return carry

        lax.fori_loop(0, per // 4, transform, 0)

    mask_wait(0)
    mask_start(1)

    def narrow(f, carry):
        spec[f] = specf[pl.ds(pl.multiple_of(f * TS, TS), TS), :].astype(jnp.bfloat16)
        return carry

    lax.fori_loop(0, FREQS, narrow, 0, unroll=8)

    mine = pl.ds(pl.multiple_of(shot * TS, TS), TS)

    def scatter(k, carry):
        ts, ty = chip_of(shot, y, k)
        pltpu.make_async_remote_copy(
            src_ref=spec.at[ty * NS + ts],
            dst_ref=grid.at[core, y, mine],
            send_sem=send1,
            recv_sem=recv1.at[y],
            device_id=(ts, ty * 2 + core),
            device_id_type=MESH,
        ).start()
        return carry

    pltpu.make_async_copy(spec.at[me], grid.at[core, y, mine], recv1.at[y]).start()
    lax.fori_loop(1, CHIPS, scatter, 0)

    mask_wait(1)
    mask_start(2)

    def slab_copy(ty):
        return pltpu.make_async_remote_copy(
            src_ref=grid.at[core, ty],
            dst_ref=grid.at[core, ty],
            send_sem=xsend.at[ty],
            recv_sem=xrecv.at[ty],
            device_id=(shot, y * 2 + 1 - core),
            device_id_type=MESH,
        )

    def forward(d, carry):
        ty = lax.rem(y + 4 - d, 4)
        pltpu.make_async_copy(grid.at[core, ty], grid.at[core, ty], recv1.at[ty]).wait()
        slab_copy(ty).start()
        return carry

    lax.fori_loop(0, NY, forward, 0)

    mask_wait(2)
    block = lax.broadcasted_iota(jnp.int32, (128, 8 * 128), 0)
    column = lax.broadcasted_iota(jnp.int32, (128, 8 * 128), 1)
    expand = jnp.where(block == 2 * (column // 128) + column % TR // TS, 1.0, 0.0).astype(jnp.bfloat16)
    mexp[...] = jnp.dot(
        mtab[...].reshape(CHIPS, 128).astype(jnp.bfloat16), expand, preferred_element_type=jnp.float32
    )

    for ty in range(NY):
        other = grid.at[1 - core, ty]
        pltpu.make_async_copy(other, other, xrecv.at[ty]).wait()

    left64 = lax.broadcasted_iota(jnp.int32, (TR, 128), 1) < TR

    def column_tile(d, carry):
        ty = lax.rem(y + d, 4)
        for j in range(8):
            part = grid[core, ty, j * TR : (j + 1) * TR, :]
            turned = pltpu.roll(part.astype(jnp.float32), TR, 1)
            rhat[j * 128 : j * 128 + TR, :] = part
            rhat[j * 128 + TR : (j + 1) * 128, :] = jnp.where(left64, -turned, turned).astype(jnp.bfloat16)

        def weigh(i, carry):
            rows = pl.ds(pl.multiple_of(i * TS, TS), TS)
            weights = mexp[pl.ds(ty * NS + i, 1), :]
            for j in range(8):
                w = jnp.broadcast_to(weights[:, j * 128 : (j + 1) * 128], (TS, 128)).astype(jnp.bfloat16)
                masked[rows, j * 128 : (j + 1) * 128] = grid[j % 2, j // 2, rows, :] * w
            return carry

        lax.fori_loop(0, NS, weigh, 0)
        prod[ty] = jnp.dot(masked[...], rhat[...], preferred_element_type=jnp.float32).astype(jnp.bfloat16)

        def give(n, carry):
            ts, ty2 = chip_of(shot, y, n * 4 + d)
            pltpu.make_async_remote_copy(
                src_ref=prod.at[ty, pl.ds(pl.multiple_of(ts * TS, TS), TS)],
                dst_ref=back.at[y, shot],
                send_sem=send2,
                recv_sem=recv2.at[d],
                device_id=(ts, ty * 2 + core),
                device_id_type=MESH,
            ).start()
            return carry

        lax.fori_loop(jnp.where(d == 0, 1, 0), NS, give, 0)
        return carry

    lax.fori_loop(0, NY, column_tile, 0)
    pltpu.make_async_copy(prod.at[y, mine], back.at[y, shot], recv2.at[0]).start()

    def collect(d, carry):
        ty = lax.rem(y + 4 - d, 4)
        pltpu.make_async_copy(back.at[ty], back.at[ty], recv2.at[d]).wait()

        def widen(n, carry):
            tile = back[ty, n].astype(jnp.float32)
            out[ty * NS + n, 0] = tile[:, :TR]
            out[ty * NS + n, 1] = pltpu.roll(tile, TR, 1)[:, :TR]
            return carry

        lax.fori_loop(0, NS, widen, 0, unroll=4)
        return carry

    lax.fori_loop(0, NY, collect, 0)

    def slab_sent(ty, carry):
        slab_copy(ty).wait_send()
        return carry

    lax.fori_loop(0, NY, slab_sent, 0)
    sent = spec.at[pl.ds(0, CHIPS - 1)]
    pltpu.make_async_copy(sent, sent, send1).wait()
    pltpu.make_async_copy(sent, sent, send2).wait()


def local(traces, aperture_lists, aperture_counts):
    bf16, f32 = jnp.bfloat16, jnp.float32
    out = pl.pallas_call(
        kernel,
        out_shape=jax.ShapeDtypeStruct((FREQS, 2, TS, TR), f32),
        in_specs=[
            pl.BlockSpec(memory_space=pl.ANY),
            pl.BlockSpec(memory_space=pl.ANY),
            pl.BlockSpec(memory_space=pltpu.SMEM),
            pl.BlockSpec(memory_space=pltpu.SMEM),
        ],
        out_specs=pl.BlockSpec(memory_space=pltpu.VMEM),
        scratch_shapes=[
            pltpu.VMEM((TS, TR, NT), bf16),
            pltpu.VMEM((128, NT), bf16),
            pltpu.VMEM((FREQS * TS, 128), f32),
            pltpu.VMEM((FREQS, TS, 128), bf16),
            pltpu.VMEM((2, NY, NS * TS, 128), bf16),
            pltpu.VMEM((CHIPS, 1, 128), f32),
            pltpu.VMEM((CHIPS, 8 * 128), f32),
            pltpu.VMEM((NS * TS, 8 * 128), bf16),
            pltpu.VMEM((8 * 128, 128), bf16),
            pltpu.VMEM((NY, NS * TS, 128), bf16),
            pltpu.VMEM((NY, NS, TS, 128), bf16),
            pltpu.SemaphoreType.DMA((CHUNKS,)),
            pltpu.SemaphoreType.DMA,
            pltpu.SemaphoreType.DMA,
            pltpu.SemaphoreType.DMA((NY,)),
            pltpu.SemaphoreType.DMA((NY,)),
            pltpu.SemaphoreType.DMA((NY,)),
            pltpu.SemaphoreType.DMA,
            pltpu.SemaphoreType.DMA((NY,)),
            pltpu.SemaphoreType.DMA((9,)),
            pltpu.SemaphoreType.DMA((9,)),
        ],
        compiler_params=pltpu.CompilerParams(
            collective_id=0, has_side_effects=True, vmem_limit_bytes=32 * 2**20
        ),
        cost_estimate=pl.CostEstimate(flops=2**30, bytes_accessed=8 * 2**20, transcendentals=0),
        name="multiples",
    )(traces, jnp.asarray(dft_table()), aperture_lists.reshape(1, APB), aperture_counts)
    return out * SCALE


def solution(mesh):
    placed = (P("shot", "rcv", None), P("shot", "rcv", None), P("shot", "rcv"))
    return jax.shard_map(
        local, mesh=mesh, in_specs=placed, out_specs=P(None, None, "shot", "rcv"), check_vma=False
    )
```

time: 239 us -> 44.7 us (0.19)
  the two profiles are of different devices: /device:TPU:0 before, /device:TPU:1 now
where the time goes in v1:
time: 44.7 us; the launch traced here: 44.6 us
  Pallas kernels  38.5 us (86%)
  local copies, waits for them, and re-layouts  3.79 us (8%)
  other arithmetic  1.55 us (3%)
  between operations  0.67 us (1%)
    pallas_call x1, Pallas kernels, local(): pl.pallas_call(kernel, out_shape=jax.ShapeDtypeStruct((FREQS, 2, TS, TR),...  38.5 us
    unnamed x6, local copies, waits for them, and re-layouts  3.79 us
    mul x1, other arithmetic, local(): return out * SCALE  1.55 us

profile of v1, /device:TPU:1, one launch (start us, length us, event | category | flops | bytes accessed | tf_op | source)
XLA Modules:
  0.0 44.6 jit_solution(16441743787919007405)
XLA Ops:
  0.7 0.0 copy-start
  0.7 2.2 %copy-done = bf16[32,64,1024]{2,1,0:T(8,128)(2,1)S(1)} copy-done((bf16[32,64,1024]{2,1,0:T(8,128)(2,1)S(1)}, bf16[32,64,1024]{2,1,0:T(8,128)(2,1)}, u32[]{:S(2)}) %copy-start) | copy-done | bytes 4194328
  2.8 0.0 copy-start.1
  2.8 0.9 %copy-done.1 = bf16[128,1024]{1,0:T(8,128)(2,1)S(1)} copy-done((bf16[128,1024]{1,0:T(8,128)(2,1)S(1)}, bf16[128,1024]{1,0:T(8,128)(2,1)}, u32[]{:S(2)}) %copy-start.1) | copy-done | bytes 262168
  3.8 0.0 copy-start.2
  3.8 0.7 %copy-done.2 = s32[1,1,8]{2,1,0:T(1,128)S(1)} copy-done((s32[1,1,8]{2,1,0:T(1,128)S(1)}, s32[1,1,8]{2,1,0:T(1,128)}, u32[]{:S(2)}) %copy-start.2) | copy-done | bytes 56
  4.4 38.5 %multiples.1 = f32[64,2,32,64]{3,2,1,0:T(8,128)S(1)} custom-call(bf16[32,64,1024]{2,1,0:T(8,128)(2,1)S(1)} %copy-done, bf16[128,1024]{1,0:T(8,128)(2,1)S(1)} %copy-done.1, s32[1,8]{1,0:T(1,128)S(1)} %bitcast.1, s32[1,1]{1,0:T(1,128)S(6)} %copy.5.counts), custom_call_target="tpu_custom_call" | custom-call | flops 1073741824 | bytes 8388608 | tf_op jit(solution)/shard_map/multiples/pallas_call | solution.py:283
  43.0 1.6 %broadcast_multiply_fusion = f32[64,2,32,64]{3,2,1,0:T(8,128)} fusion(f32[64,2,32,64]{3,2,1,0:T(8,128)S(1)} %multiples.1), kind=kLoop, calls=%fused_computation | loop fusion | flops 262144 | bytes 2097152 | tf_op jit(solution)/shard_map/mul | solution.py:322
Async XLA Ops:
  0.7 2.2 %copy-start = (bf16[32,64,1024]{2,1,0:T(8,128)(2,1)S(1)}, bf16[32,64,1024]{2,1,0:T(8,128)(2,1)}, u32[]{:S(2)}) copy-start(bf16[32,64,1024]{2,1,0:T(8,128)(2,1)} %traces.1) | copy-start | bytes 12582916
  2.8 0.9 %copy-start.1 = (bf16[128,1024]{1,0:T(8,128)(2,1)S(1)}, bf16[128,1024]{1,0:T(8,128)(2,1)}, u32[]{:S(2)}) copy-start(bf16[128,1024]{1,0:T(8,128)(2,1)} %constant.4.clone.table_hbm) | copy-start | bytes 786436
  3.8 0.7 %copy-start.2 = (s32[1,1,8]{2,1,0:T(1,128)S(1)}, s32[1,1,8]{2,1,0:T(1,128)}, u32[]{:S(2)}) copy-start(s32[1,1,8]{2,1,0:T(1,128)} %param.5) | copy-start | bytes 100

commit v2 on v1

v2 whole, which is shorter than its diff:
```python
import math

import jax
import jax.numpy as jnp
import ml_dtypes
import numpy as np
from jax import lax
from jax.experimental import pallas as pl
from jax.experimental.pallas import tpu as pltpu
from jax.sharding import PartitionSpec as P

MESH = pl.DeviceIdType.MESH

NT = 1024
BAND = 32
APB = 8
FIRST = 32
SECOND = 128
FREQS = 64
TS = 32
TR = 64
NS = 16
NY = 4
CHIPS = 64
SCALE = 1.0 / math.sqrt(APB * TS)
CHUNKS = 2
PITCH = 40
VMEM_MIB = 50
ORDER = sorted(
    [(a, b, c) for a in range(4) for b in range(4) for c in range(4) if a or b or c],
    key=lambda k: sum(min(d, 4 - d) for d in k),
)
BACK = (2, 1, 3, 0)


def dft_table():
    sample = np.arange(NT)
    bins = np.concatenate([FIRST + np.arange(BAND), SECOND + np.arange(BAND)])
    phase = (bins[:, None] * sample[None, :] % NT).astype(np.float32) * np.float32(2.0 * math.pi / NT)
    phase = phase.astype(np.float64)
    factor = 1.0 / math.sqrt(NT)
    return (np.concatenate([np.cos(phase), -np.sin(phase)], axis=0) * factor).astype(np.float32).astype(
        ml_dtypes.bfloat16
    )


def kernel(
    traces,
    table_hbm,
    lists_hbm,
    counts_hbm,
    out,
    tr,
    table,
    lists,
    counts,
    specf,
    spec,
    grid,
    mtab,
    mrow,
    mask,
    masked,
    rhat,
    acc,
    prod,
    back,
    load_sem,
    table_sem,
    small_sem,
    send1,
    recv1,
    xsend,
    xrecv,
    send2,
    recv2,
    msend,
    mrecv,
):
    shot = lax.axis_index("shot")
    rcv = lax.axis_index("rcv")
    y = rcv // 2
    core = rcv % 2
    z, x = shot // 4, shot % 4
    me = y * NS + shot
    sibling = (shot, y * 2 + 1 - core)
    zs = [(z + d) % 4 * 4 for d in range(4)]
    xs = [(x + d) % 4 for d in range(4)]
    ys = [(y + d) % 4 for d in range(4)]

    per = TS // CHUNKS
    loads = [
        pltpu.make_async_copy(traces.at[pl.ds(n * per, per)], tr.at[pl.ds(n * per, per)], load_sem.at[n])
        for n in range(CHUNKS)
    ]
    table_load = pltpu.make_async_copy(table_hbm, table, table_sem)
    lists_load = pltpu.make_async_copy(lists_hbm, lists, small_sem.at[0])
    counts_load = pltpu.make_async_copy(counts_hbm, counts, small_sem.at[1])
    table_load.start()
    for load in loads:
        load.start()
    lists_load.start()
    counts_load.start()

    barrier = pltpu.get_barrier_semaphore()
    pl.semaphore_signal(barrier, inc=1, device_id=sibling, device_id_type=MESH)
    for dz, dx, dy in ORDER:
        pl.semaphore_signal(
            barrier, inc=1, device_id=(zs[dz] + xs[dx], ys[dy] * 2 + core), device_id_type=MESH
        )

    lists_load.wait()
    counts_load.wait()
    lane = lax.broadcasted_iota(jnp.int32, (1, 128), 1)
    live = counts[0, 0]
    member = jnp.zeros((1, 128), jnp.float32)
    for k in range(APB):
        block = jnp.where(k < live, lists[0, 0, k], -1)
        member = jnp.where(lane == block, 1.0, member)
    mtab[me] = member

    low = lax.broadcasted_iota(jnp.int32, (FREQS, 128), 1) < TR
    table_load.wait()
    for n in range(CHUNKS):
        loads[n].wait()
        rows = tr[n * per : (n + 1) * per].reshape(per * TR, NT)
        flat = lax.dot_general(
            table[...], rows, (((1,), (1,)), ((), ())), preferred_element_type=jnp.float32
        )
        for p in range(per // 2):
            first = n * per + 2 * p
            re = flat[:FREQS, p * 128 : p * 128 + 128]
            im = flat[FREQS:, p * 128 : p * 128 + 128]
            specf[pl.ds(first, FREQS, stride=PITCH), :] = jnp.where(low, re, pltpu.roll(im, TR, 1))
            specf[pl.ds(first + 1, FREQS, stride=PITCH), :] = jnp.where(low, pltpu.roll(re, TR, 1), im)
    spec[...] = specf[...].reshape(FREQS, PITCH, 128)[:, :TS].astype(jnp.bfloat16)

    def mask_copy(stage, d):
        if stage == 0:
            rows, to = pl.ds(me, 1), (zs[0] + xs[d], rcv)
        elif stage == 1:
            rows, to = pl.ds(y * NS + z * 4, 4), (zs[d] + x, rcv)
        else:
            rows, to = pl.ds(y * NS, NS), (shot, ys[d] * 2 + core)
        return pltpu.make_async_remote_copy(
            src_ref=mtab.at[rows],
            dst_ref=mtab.at[rows],
            send_sem=msend.at[stage * 3 + d - 1],
            recv_sem=mrecv.at[stage * 3 + d - 1],
            device_id=to,
            device_id_type=MESH,
        )

    def mask_start(stage):
        for d in (1, 2, 3):
            mask_copy(stage, d).start()

    def mask_wait(stage):
        for d in (1, 2, 3):
            mask_copy(stage, d).wait()

    mine = pl.ds(pl.multiple_of(shot * TS, TS), TS)

    def scatter(dz, dx, dy):
        ts = zs[dz] + xs[dx]
        pltpu.make_async_remote_copy(
            src_ref=spec.at[ys[dy] * NS + ts],
            dst_ref=grid.at[core, y, mine],
            send_sem=send1,
            recv_sem=recv1.at[y],
            device_id=(ts, ys[dy] * 2 + core),
            device_id_type=MESH,
        ).start()

    pl.semaphore_wait(barrier, CHIPS)
    mask_start(0)
    for step in ORDER[:32]:
        scatter(*step)
    mask_wait(0)
    mask_start(1)
    for step in ORDER[32:]:
        scatter(*step)
    pltpu.make_async_copy(spec.at[me], grid.at[core, y, mine], recv1.at[y]).start()
    mask_wait(1)
    mask_start(2)

    block = lax.broadcasted_iota(jnp.int32, (128, 1024), 0)
    column = lax.broadcasted_iota(jnp.int32, (128, 1024), 1)
    tile = column % 512 // 128 * 2 + (column // 512 + core) % 2
    expand = jnp.where(block == 2 * tile + column % TR // TS, 1.0, 0.0).astype(jnp.bfloat16)
    mask_wait(2)
    mrow[...] = jnp.dot(
        mtab[...].reshape(CHIPS, 128).astype(jnp.bfloat16), expand, preferred_element_type=jnp.float32
    )

    def spread(t, carry):
        mask[t] = jnp.broadcast_to(mrow[pl.ds(t, 1), :], (16, 1024)).astype(jnp.bfloat16)
        return carry

    lax.fori_loop(0, CHIPS, spread, 0, unroll=4)

    def slab_copy(ty):
        return pltpu.make_async_remote_copy(
            src_ref=grid.at[core, ty],
            dst_ref=grid.at[core, ty],
            send_sem=xsend.at[ty],
            recv_sem=xrecv.at[ty],
            device_id=sibling,
            device_id_type=MESH,
        )

    for d in (0, 3, 2, 1):
        slab = grid.at[core, ys[d]]
        pltpu.make_async_copy(slab, slab, recv1.at[ys[d]]).wait()
        slab_copy(ys[d]).start()

    left64 = lax.broadcasted_iota(jnp.int32, (TR, 128), 1) < TR

    def half(d, h):
        par = core if h == 0 else 1 - core
        for k in range(NY):
            cols = slice(k * 128, k * 128 + 128)
            left = grid[par, k].reshape(NS, 2, 16, 128)
            weights = mask[pl.ds(ys[d] * NS, NS), :, h * 512 + k * 128 : h * 512 + k * 128 + 128]
            masked[:, cols] = (left * weights[:, None]).reshape(NS * TS, 128)
            first = pl.multiple_of((2 * k + par) * TR, TR)
            part = grid[core, ys[d], pl.ds(first, TR), :]
            turned = pltpu.roll(part.astype(jnp.float32), TR, 1)
            rhat[k * 128 : k * 128 + TR, :] = part
            rhat[k * 128 + TR : (k + 1) * 128, :] = jnp.where(left64, -turned, turned).astype(jnp.bfloat16)
        return jnp.dot(masked[...], rhat[...], preferred_element_type=jnp.float32)

    for d in range(NY):
        acc[d] = half(d, 0)
    for k in range(NY):
        other = grid.at[1 - core, k]
        pltpu.make_async_copy(other, other, xrecv.at[k]).wait()
    for d in BACK:
        ty = ys[d]
        prod[ty] = (acc[d] + half(d, 1)).astype(jnp.bfloat16)
        for dz in range(4):
            for dx in range(4):
                if d or dz or dx:
                    ts = zs[dz] + xs[dx]
                    pltpu.make_async_remote_copy(
                        src_ref=prod.at[ty, pl.ds(pl.multiple_of(ts * TS, TS), TS)],
                        dst_ref=back.at[y, shot],
                        send_sem=send2,
                        recv_sem=recv2.at[d],
                        device_id=(ts, ty * 2 + core),
                        device_id_type=MESH,
                    ).start()
                else:
                    pltpu.make_async_copy(prod.at[y, mine], back.at[y, shot], recv2.at[0]).start()

    for d in BACK:
        ty = ys[-d % 4]
        pltpu.make_async_copy(back.at[ty], back.at[ty], recv2.at[d]).wait()

        def widen(n, carry):
            tile = back[ty, n].astype(jnp.float32)
            out[ty * NS + n, 0] = tile[:, :TR]
            out[ty * NS + n, 1] = pltpu.roll(tile, TR, 1)[:, :TR]
            return carry

        lax.fori_loop(0, NS, widen, 0, unroll=True)

    for k in range(NY):
        slab_copy(k).wait_send()
    sent = spec.at[pl.ds(0, CHIPS - 1)]
    pltpu.make_async_copy(sent, sent, send1).wait()
    pltpu.make_async_copy(sent, sent, send2).wait()


def local(traces, aperture_lists, aperture_counts):
    bf16, f32 = jnp.bfloat16, jnp.float32
    dma = pltpu.SemaphoreType.DMA
    out = pl.pallas_call(
        kernel,
        out_shape=jax.ShapeDtypeStruct((FREQS, 2, TS, TR), f32),
        in_specs=[pl.BlockSpec(memory_space=pl.ANY)] * 4,
        out_specs=pl.BlockSpec(memory_space=pltpu.VMEM),
        scratch_shapes=[
            pltpu.VMEM((TS, TR, NT), bf16),
            pltpu.VMEM((128, NT), bf16),
            pltpu.SMEM((1, 1, APB), jnp.int32),
            pltpu.SMEM((1, 1), jnp.int32),
            pltpu.VMEM((FREQS * PITCH, 128), f32),
            pltpu.VMEM((FREQS, TS, 128), bf16),
            pltpu.VMEM((2, NY, NS * TS, 128), bf16),
            pltpu.VMEM((CHIPS, 1, 128), f32),
            pltpu.VMEM((CHIPS, 1024), f32),
            pltpu.VMEM((CHIPS, 16, 1024), bf16),
            pltpu.VMEM((NS * TS, 512), bf16),
            pltpu.VMEM((512, 128), bf16),
            pltpu.VMEM((NY, NS * TS, 128), f32),
            pltpu.VMEM((NY, NS * TS, 128), bf16),
            pltpu.VMEM((NY, NS, TS, 128), bf16),
            dma((CHUNKS,)),
            dma,
            dma((2,)),
            dma,
            dma((NY,)),
            dma((NY,)),
            dma((NY,)),
            dma,
            dma((NY,)),
            dma((9,)),
            dma((9,)),
        ],
        compiler_params=pltpu.CompilerParams(
            collective_id=0, has_side_effects=True, vmem_limit_bytes=int(VMEM_MIB * 2**20)
        ),
        cost_estimate=pl.CostEstimate(flops=2**30, bytes_accessed=8 * 2**20, transcendentals=0),
        name="multiples",
    )(traces, jnp.asarray(dft_table()), aperture_lists, aperture_counts)
    return out * SCALE


def solution(mesh):
    placed = (P("shot", "rcv", None), P("shot", "rcv", None), P("shot", "rcv"))
    return jax.shard_map(
        local, mesh=mesh, in_specs=placed, out_specs=P(None, None, "shot", "rcv"), check_vma=False
    )
```

time: 44.7 us -> 38.1 us (0.85)
  Pallas kernels: 38.5 us -> 34.1 us
  local copies, waits for them, and re-layouts: 3.79 us -> 1.6 us
    pallas_call x1, Pallas kernels: 38.5 us -> 34.1 us  [local(): pl.pallas_call(kernel, out_shape=jax.ShapeDtypeStruct((FREQS, 2, TS, TR),...]
    unnamed x6 -> x4, local copies, waits for them, and re-layouts: 3.79 us -> 1.6 us
where the time goes in v2:
time: 38.1 us; the launch traced here: 37.9 us
  Pallas kernels  34.1 us (90%)
  local copies, waits for them, and re-layouts  1.6 us (4%)
  other arithmetic  1.55 us (4%)
  between operations  0.67 us (2%)
    pallas_call x1, Pallas kernels, local(): pl.pallas_call(kernel, out_shape=jax.ShapeDtypeStruct((FREQS, 2, TS, TR),...  34.1 us
    unnamed x4, local copies, waits for them, and re-layouts  1.6 us
    mul x1, other arithmetic, local(): return out * SCALE  1.55 us

profile of v2, /device:TPU:1, one launch (start us, length us, event | category | flops | bytes accessed | tf_op | source)
XLA Modules:
  0.0 37.9 jit_solution(430171251333621849)
XLA Ops:
  0.7 0.0 copy-start
  0.7 0.9 %copy-done = bf16[128,1024]{1,0:T(8,128)(2,1)S(1)} copy-done((bf16[128,1024]{1,0:T(8,128)(2,1)S(1)}, bf16[128,1024]{1,0:T(8,128)(2,1)}, u32[]{:S(2)}) %copy-start) | copy-done | bytes 262168
  1.6 0.0 copy-start.1
  1.6 0.7 %copy-done.1 = s32[1,1,8]{2,1,0:T(1,128)S(1)} copy-done((s32[1,1,8]{2,1,0:T(1,128)S(1)}, s32[1,1,8]{2,1,0:T(1,128)}, u32[]{:S(2)}) %copy-start.1) | copy-done | bytes 56
  2.3 34.1 %multiples.1 = f32[64,2,32,64]{3,2,1,0:T(8,128)S(1)} custom-call(bf16[32,64,1024]{2,1,0:T(8,128)(2,1)} %traces.1, bf16[128,1024]{1,0:T(8,128)(2,1)S(1)} %copy-done, s32[1,1,8]{2,1,0:T(1,128)S(1)} %copy-done.1, s32[1,1]{1,0:T(1,128)S(6)} %copy.5.counts_hbm), custom_call_target="tpu_custom_call" | custom-call | flops 1073741824 | bytes 8388608 | tf_op jit(solution)/shard_map/multiples/pallas_call | solution.py:278
  36.4 1.6 %broadcast_multiply_fusion = f32[64,2,32,64]{3,2,1,0:T(8,128)} fusion(f32[64,2,32,64]{3,2,1,0:T(8,128)S(1)} %multiples.1), kind=kLoop, calls=%fused_computation | loop fusion | flops 262144 | bytes 2097152 | tf_op jit(solution)/shard_map/mul | solution.py:317
Async XLA Ops:
  0.7 1.0 %copy-start = (bf16[128,1024]{1,0:T(8,128)(2,1)S(1)}, bf16[128,1024]{1,0:T(8,128)(2,1)}, u32[]{:S(2)}) copy-start(bf16[128,1024]{1,0:T(8,128)(2,1)} %constant.4.clone.table_hbm) | copy-start | bytes 786436
  1.6 0.7 %copy-start.1 = (s32[1,1,8]{2,1,0:T(1,128)S(1)}, s32[1,1,8]{2,1,0:T(1,128)}, u32[]{:S(2)}) copy-start(s32[1,1,8]{2,1,0:T(1,128)} %lists_hbm.1) | copy-start | bytes 100

commit v3 on v2

v3 whole, which is shorter than its diff:
```python
import math

import jax
import jax.numpy as jnp
import ml_dtypes
import numpy as np
from jax import lax
from jax.experimental import pallas as pl
from jax.experimental.pallas import tpu as pltpu
from jax.sharding import PartitionSpec as P

MESH = pl.DeviceIdType.MESH

NT = 1024
BAND = 32
APB = 8
FIRST = 32
SECOND = 128
FREQS = 64
TS = 32
TR = 64
NS = 16
NY = 4
CHIPS = 64
SCALE = 1.0 / math.sqrt(APB * TS)
CHUNKS = 2
PITCH = 40
VMEM_MIB = 60
BACK = (2, 1, 3, 0)
PLANE = [(a, b) for a in (2, 1, 3, 0) for b in (2, 1, 3, 0)]


def dft_table():
    sample = np.arange(NT)
    bins = np.concatenate([FIRST + np.arange(BAND), SECOND + np.arange(BAND)])
    phase = (bins[:, None] * sample[None, :] % NT).astype(np.float32) * np.float32(2.0 * math.pi / NT)
    phase = phase.astype(np.float64)
    factor = 1.0 / math.sqrt(NT)
    return (np.concatenate([np.cos(phase), -np.sin(phase)], axis=0) * factor).astype(np.float32).astype(
        ml_dtypes.bfloat16
    )


def kernel(
    traces,
    table_hbm,
    lists_hbm,
    back,
    tr,
    table,
    lists,
    specf,
    spec,
    grid,
    mtab,
    mrow,
    mask,
    masked,
    rhat,
    acc,
    prod,
    load_sem,
    table_sem,
    small_sem,
    send1,
    recv1,
    xsend,
    xrecv,
    send2,
    recv2,
    msend,
    mrecv,
    ready,
):
    shot = lax.axis_index("shot")
    rcv = lax.axis_index("rcv")
    y = rcv // 2
    core = rcv % 2
    z, x = shot // 4, shot % 4
    me = y * NS + shot
    sibling = (shot, y * 2 + 1 - core)
    zs = [(z + d) % 4 * 4 for d in range(4)]
    xs = [(x + d) % 4 for d in range(4)]
    ys = [(y + d) % 4 for d in range(4)]

    per = TS // CHUNKS
    loads = [
        pltpu.make_async_copy(traces.at[pl.ds(n * per, per)], tr.at[pl.ds(n * per, per)], load_sem.at[n])
        for n in range(CHUNKS)
    ]
    table_load = pltpu.make_async_copy(table_hbm, table, table_sem)
    lists_load = pltpu.make_async_copy(lists_hbm, lists, small_sem)
    table_load.start()
    for load in loads:
        load.start()
    lists_load.start()

    barrier = pltpu.get_barrier_semaphore()
    pl.semaphore_signal(barrier, inc=1, device_id=sibling, device_id_type=MESH)
    for d in (1, 2, 3):
        pl.semaphore_signal(barrier, inc=1, device_id=(zs[d] + x, rcv), device_id_type=MESH)
    for dx, dy in PLANE:
        if dx or dy:
            pl.semaphore_signal(
                barrier, inc=1, device_id=(z * 4 + xs[dx], ys[dy] * 2 + core), device_id_type=MESH
            )

    lists_load.wait()
    lane = lax.broadcasted_iota(jnp.int32, (1, 128), 1)
    member = jnp.where(lane == lists[0, 0, 0], 1.0, 0.0)
    for k in range(1, APB):
        entry = lists[0, 0, k]
        block = jnp.where(entry == 0, -1, entry)
        member = jnp.where(lane == block, 1.0, member)
    mrank = shot * NY + y
    mtab[mrank] = member

    low = lax.broadcasted_iota(jnp.int32, (FREQS, 128), 1) < TR
    table_load.wait()
    for n in range(CHUNKS):
        loads[n].wait()
        rows = tr[n * per : (n + 1) * per].reshape(per * TR, NT)
        flat = lax.dot_general(
            table[...], rows, (((1,), (1,)), ((), ())), preferred_element_type=jnp.float32
        )
        for p in range(per // 2):
            first = n * per + 2 * p
            re = flat[:FREQS, p * 128 : p * 128 + 128]
            im = flat[FREQS:, p * 128 : p * 128 + 128]
            specf[pl.ds(first, FREQS, stride=PITCH), :] = jnp.where(low, re, pltpu.roll(im, TR, 1))
            specf[pl.ds(first + 1, FREQS, stride=PITCH), :] = jnp.where(low, pltpu.roll(re, TR, 1), im)
    spec[...] = specf[...].reshape(FREQS, PITCH, 128)[:, :TS].astype(jnp.bfloat16)

    def mask_copy(d):
        return pltpu.make_async_remote_copy(
            src_ref=mtab.at[pl.ds(z * NS, NS)],
            dst_ref=mtab.at[pl.ds(z * NS, NS)],
            send_sem=msend.at[NS - 1 + d],
            recv_sem=mrecv.at[NS - 1 + d],
            device_id=(zs[d] + x, rcv),
            device_id_type=MESH,
        )

    def mask_start():
        for d in (1, 2, 3):
            mask_copy(d).start()

    def mask_wait():
        for d in (1, 2, 3):
            mask_copy(d).wait()

    def plane_copy(dx, dy):
        return pltpu.make_async_remote_copy(
            src_ref=mtab.at[pl.ds(mrank, 1)],
            dst_ref=mtab.at[pl.ds(mrank, 1)],
            send_sem=msend.at[dx * 4 + dy],
            recv_sem=mrecv.at[dx * 4 + dy],
            device_id=(z * 4 + xs[dx], ys[dy] * 2 + core),
            device_id_type=MESH,
        )

    def plane_start():
        for k in range(1, NS):
            plane_copy(k // 4, k % 4).start()

    def plane_wait():
        for k in range(1, NS):
            plane_copy(k // 4, k % 4).wait()

    mine = pl.ds(pl.multiple_of(shot * TS, TS), TS)

    def scatter(plane, dx, dy):
        ts = plane * 4 + xs[dx]
        pltpu.make_async_remote_copy(
            src_ref=spec.at[ys[dy] * NS + ts],
            dst_ref=grid.at[core, y, mine],
            send_sem=send1,
            recv_sem=recv1.at[y],
            device_id=(ts, ys[dy] * 2 + core),
            device_id_type=MESH,
        ).start()

    pl.semaphore_wait(barrier, NS + 3)
    for d in (1, 2, 3):
        pl.semaphore_signal(ready.at[z], inc=1, device_id=(zs[d] + x, rcv), device_id_type=MESH)
    plane_start()
    for dx, dy in PLANE:
        if dx or dy:
            scatter(z, dx, dy)
    pltpu.make_async_copy(spec.at[me], grid.at[core, y, mine], recv1.at[y]).start()
    for k in range(3):
        plane = (z + (2, 1, 3)[k]) % 4
        pl.semaphore_wait(ready.at[plane], 1)
        for dx, dy in PLANE:
            scatter(plane, dx, dy)
    plane_wait()
    mask_start()

    block = lax.broadcasted_iota(jnp.int32, (128, 1024), 0)
    column = lax.broadcasted_iota(jnp.int32, (128, 1024), 1)
    tile = column % 512 // 128 * 2 + (column // 512 + core) % 2
    expand = jnp.where(block == 2 * tile + column % TR // TS, 1.0, 0.0).astype(jnp.bfloat16)
    def slab_copy(ty):
        return pltpu.make_async_remote_copy(
            src_ref=grid.at[core, ty],
            dst_ref=grid.at[core, ty],
            send_sem=xsend.at[ty],
            recv_sem=xrecv.at[ty],
            device_id=sibling,
            device_id_type=MESH,
        )

    for d in (0, 3, 2, 1):
        slab = grid.at[core, ys[d]]
        pltpu.make_async_copy(slab, slab, recv1.at[ys[d]]).wait()
        slab_copy(ys[d]).start()

    mask_wait()
    mrow[...] = jnp.dot(
        mtab[...].reshape(CHIPS, 128).astype(jnp.bfloat16), expand, preferred_element_type=jnp.float32
    )

    def spread(t, carry):
        mask[t % NY, t // NY] = jnp.broadcast_to(mrow[pl.ds(t, 1), :], (16, 1024)).astype(jnp.bfloat16)
        return carry

    lax.fori_loop(0, CHIPS, spread, 0, unroll=4)

    left64 = lax.broadcasted_iota(jnp.int32, (TR, 128), 1) < TR

    def half(d, h):
        par = core if h == 0 else 1 - core
        for k in range(NY):
            cols = slice(k * 128, k * 128 + 128)
            left = grid[par, k].reshape(NS, 2, 16, 128)
            weights = mask[ys[d], :, :, h * 512 + k * 128 : h * 512 + k * 128 + 128]
            masked[:, cols] = (left * weights[:, None]).reshape(NS * TS, 128)
            first = pl.multiple_of((2 * k + par) * TR, TR)
            part = grid[core, ys[d], pl.ds(first, TR), :]
            turned = pltpu.roll(part.astype(jnp.float32), TR, 1)
            rhat[k * 128 : k * 128 + TR, :] = part
            rhat[k * 128 + TR : (k + 1) * 128, :] = jnp.where(left64, -turned, turned).astype(jnp.bfloat16)
        return jnp.dot(masked[...], rhat[...], preferred_element_type=jnp.float32)

    for d in range(NY):
        acc[d] = half(d, 0)
    for k in range(NY):
        other = grid.at[1 - core, k]
        pltpu.make_async_copy(other, other, xrecv.at[k]).wait()
    for d in BACK:
        ty = ys[d]
        prod[ty] = (acc[d] + half(d, 1)).astype(jnp.bfloat16)
        for dz, dx in PLANE:
            if d or dz or dx:
                ts = zs[dz] + xs[dx]
                pltpu.make_async_remote_copy(
                    src_ref=prod.at[ty, pl.ds(pl.multiple_of(ts * TS, TS), TS)],
                    dst_ref=back.at[y, shot],
                    send_sem=send2,
                    recv_sem=recv2.at[d],
                    device_id=(ts, ty * 2 + core),
                    device_id_type=MESH,
                ).start()
            else:
                pltpu.make_async_copy(prod.at[y, mine], back.at[y, shot], recv2.at[0]).start()

    for d in BACK:
        ty = ys[-d % 4]
        pltpu.make_async_copy(back.at[ty], back.at[ty], recv2.at[d]).wait()

    for k in range(NY):
        slab_copy(k).wait_send()
    sent = spec.at[pl.ds(0, CHIPS - 1)]
    pltpu.make_async_copy(sent, sent, send1).wait()
    pltpu.make_async_copy(sent, sent, send2).wait()


def widen(back, out, tiles, wide, in_sem, out_sem):
    loads = [pltpu.make_async_copy(back.at[k], tiles.at[k], in_sem.at[k]) for k in range(NY)]
    for load in loads:
        load.start()
    stores = []
    for k in range(NY):
        part = pl.ds(k * NS, NS)
        loads[k].wait()
        for n in range(NS):
            tile = tiles[k, n].astype(jnp.float32) * SCALE
            wide[k * NS + n, 0] = tile[:, :TR]
            wide[k * NS + n, 1] = pltpu.roll(tile, TR, 1)[:, :TR]
        stores.append(pltpu.make_async_copy(wide.at[part], out.at[part], out_sem.at[k]))
        stores[k].start()
    for store in stores:
        store.wait()


def local(traces, aperture_lists, aperture_counts):
    bf16, f32 = jnp.bfloat16, jnp.float32
    dma = pltpu.SemaphoreType.DMA
    back = pl.pallas_call(
        kernel,
        out_shape=jax.ShapeDtypeStruct((NY, NS, TS, 128), bf16),
        in_specs=[pl.BlockSpec(memory_space=pl.ANY)] * 3,
        out_specs=pl.BlockSpec(memory_space=pl.ANY),
        scratch_shapes=[
            pltpu.VMEM((TS, TR, NT), bf16),
            pltpu.VMEM((128, NT), bf16),
            pltpu.SMEM((1, 1, APB), jnp.int32),
            pltpu.VMEM((FREQS * PITCH, 128), f32),
            pltpu.VMEM((FREQS, TS, 128), bf16),
            pltpu.VMEM((2, NY, NS * TS, 128), bf16),
            pltpu.VMEM((CHIPS, 1, 128), f32),
            pltpu.VMEM((CHIPS, 1024), f32),
            pltpu.VMEM((NY, NS, 16, 1024), bf16),
            pltpu.VMEM((NS * TS, 512), bf16),
            pltpu.VMEM((512, 128), bf16),
            pltpu.VMEM((NY, NS * TS, 128), f32),
            pltpu.VMEM((NY, NS * TS, 128), bf16),
            dma((CHUNKS,)),
            dma,
            dma,
            dma,
            dma((NY,)),
            dma((NY,)),
            dma((NY,)),
            dma,
            dma((NY,)),
            dma((19,)),
            dma((19,)),
            pltpu.SemaphoreType.REGULAR((4,)),
        ],
        compiler_params=pltpu.CompilerParams(
            collective_id=0, has_side_effects=True, vmem_limit_bytes=int(VMEM_MIB * 2**20)
        ),
        cost_estimate=pl.CostEstimate(flops=2**30, bytes_accessed=8 * 2**20, transcendentals=0),
        name="multiples",
    )(traces, jnp.asarray(dft_table()), aperture_lists)
    return pl.pallas_call(
        widen,
        out_shape=jax.ShapeDtypeStruct((FREQS, 2, TS, TR), f32),
        in_specs=[pl.BlockSpec(memory_space=pl.ANY)],
        out_specs=pl.BlockSpec(memory_space=pl.ANY),
        scratch_shapes=[
            pltpu.VMEM((NY, NS, TS, 128), bf16),
            pltpu.VMEM((FREQS, 2, TS, TR), f32),
            dma((NY,)),
            dma((NY,)),
        ],
        compiler_params=pltpu.CompilerParams(vmem_limit_bytes=int(VMEM_MIB * 2**20)),
        cost_estimate=pl.CostEstimate(flops=2**20, bytes_accessed=3 * 2**20, transcendentals=0),
        name="widen",
    )(back)


def solution(mesh):
    placed = (P("shot", "rcv", None), P("shot", "rcv", None), P("shot", "rcv"))
    return jax.shard_map(
        local, mesh=mesh, in_specs=placed, out_specs=P(None, None, "shot", "rcv"), check_vma=False
    )
```

time: 38.1 us -> 33.2 us (0.87)
  the two profiles are of different devices: /device:TPU:1 before, /device:TPU:0 now
where the time goes in v3:
time: 33.2 us; the launch traced here: 33.1 us
  Pallas kernels  33.1 us (100%)
    pallas_call x1, Pallas kernels, local(): pl.pallas_call(kernel, out_shape=jax.ShapeDtypeStruct((NY, NS, TS, 128),...  30.7 us
    pallas_call x1, Pallas kernels, local(): pl.pallas_call(widen, out_shape=jax.ShapeDtypeStruct((FREQS, 2, TS, TR),...  2.42 us

profile of v3, /device:TPU:0, one launch (start us, length us, event | category | flops | bytes accessed | tf_op | source)
XLA Modules:
  0.0 33.1 jit_solution(11254732802797505432)
XLA Ops:
  0.0 30.7 %multiples.1.back = bf16[4,16,32,128]{3,2,1,0:T(8,128)(2,1)} custom-call(bf16[32,64,1024]{2,1,0:T(8,128)(2,1)} %traces.1, bf16[128,1024]{1,0:T(8,128)(2,1)} %constant.2.clone.table_hbm, s32[1,1,8]{2,1,0:T(1,128)} %lists_hbm.1), custom_call_target="tpu_custom_call" | custom-call | flops 1073741824 | bytes 8388608 | tf_op jit(solution)/shard_map/multiples/pallas_call | solution.py:299
  30.7 2.4 %widen.1 = f32[64,2,32,64]{3,2,1,0:T(8,128)} custom-call(bf16[4,16,32,128]{3,2,1,0:T(8,128)(2,1)} %multiples.1.back), custom_call_target="tpu_custom_call" | custom-call | flops 1048576 | bytes 3145728 | tf_op jit(solution)/shard_map/widen/pallas_call | solution.py:337

commit v4 on v3

--- a/solution.py
+++ b/solution.py
@@ -98,11 +98,13 @@
     barrier = pltpu.get_barrier_semaphore()
     pl.semaphore_signal(barrier, inc=1, device_id=sibling, device_id_type=MESH)
     for d in (1, 2, 3):
-        pl.semaphore_signal(barrier, inc=1, device_id=(zs[d] + x, rcv), device_id_type=MESH)
-    for dx, dy in PLANE:
-        if dx or dy:
+        pl.semaphore_signal(
+            barrier, inc=1, device_id=(shot, ys[d] * 2 + core), device_id_type=MESH
+        )
+    for dz, dx in PLANE:
+        if dz or dx:
             pl.semaphore_signal(
-                barrier, inc=1, device_id=(z * 4 + xs[dx], ys[dy] * 2 + core), device_id_type=MESH
+                barrier, inc=1, device_id=(zs[dz] + xs[dx], rcv), device_id_type=MESH
             )
 
     lists_load.wait()
@@ -112,8 +114,7 @@
         entry = lists[0, 0, k]
         block = jnp.where(entry == 0, -1, entry)
         member = jnp.where(lane == block, 1.0, member)
-    mrank = shot * NY + y
-    mtab[mrank] = member
+    mtab[me] = member
 
     low = lax.broadcasted_iota(jnp.int32, (FREQS, 128), 1) < TR
     table_load.wait()
@@ -131,70 +132,59 @@
             specf[pl.ds(first + 1, FREQS, stride=PITCH), :] = jnp.where(low, pltpu.roll(re, TR, 1), im)
     spec[...] = specf[...].reshape(FREQS, PITCH, 128)[:, :TS].astype(jnp.bfloat16)
 
-    def mask_copy(d):
+    def mask_copy(stage, d):
+        if stage == 0:
+            rows, to = pl.ds(me, 1), (zs[0] + xs[d], rcv)
+        elif stage == 1:
+            rows, to = pl.ds(y * NS + z * 4, 4), (zs[d] + x, rcv)
+        else:
+            rows, to = pl.ds(y * NS, NS), (shot, ys[d] * 2 + core)
         return pltpu.make_async_remote_copy(
-            src_ref=mtab.at[pl.ds(z * NS, NS)],
-            dst_ref=mtab.at[pl.ds(z * NS, NS)],
-            send_sem=msend.at[NS - 1 + d],
-            recv_sem=mrecv.at[NS - 1 + d],
-            device_id=(zs[d] + x, rcv),
+            src_ref=mtab.at[rows],
+            dst_ref=mtab.at[rows],
+            send_sem=msend.at[stage * 3 + d - 1],
+            recv_sem=mrecv.at[stage * 3 + d - 1],
+            device_id=to,
             device_id_type=MESH,
         )
 
-    def mask_start():
+    def mask_start(stage):
         for d in (1, 2, 3):
-            mask_copy(d).start()
-
-    def mask_wait():
+            mask_copy(stage, d).start()
+
+    def mask_wait(stage):
         for d in (1, 2, 3):
-            mask_copy(d).wait()
-
-    def plane_copy(dx, dy):
-        return pltpu.make_async_remote_copy(
-            src_ref=mtab.at[pl.ds(mrank, 1)],
-            dst_ref=mtab.at[pl.ds(mrank, 1)],
-            send_sem=msend.at[dx * 4 + dy],
-            recv_sem=mrecv.at[dx * 4 + dy],
-            device_id=(z * 4 + xs[dx], ys[dy] * 2 + core),
-            device_id_type=MESH,
-        )
-
-    def plane_start():
-        for k in range(1, NS):
-            plane_copy(k // 4, k % 4).start()
-
-    def plane_wait():
-        for k in range(1, NS):
-            plane_copy(k // 4, k % 4).wait()
+            mask_copy(stage, d).wait()
 
     mine = pl.ds(pl.multiple_of(shot * TS, TS), TS)
 
-    def scatter(plane, dx, dy):
-        ts = plane * 4 + xs[dx]
+    def scatter(plane, dz, dx):
+        ts = zs[dz] + xs[dx]
         pltpu.make_async_remote_copy(
-            src_ref=spec.at[ys[dy] * NS + ts],
+            src_ref=spec.at[plane * NS + ts],
             dst_ref=grid.at[core, y, mine],
             send_sem=send1,
             recv_sem=recv1.at[y],
-            device_id=(ts, ys[dy] * 2 + core),
+            device_id=(ts, plane * 2 + core),
             device_id_type=MESH,
         ).start()
 
     pl.semaphore_wait(barrier, NS + 3)
     for d in (1, 2, 3):
-        pl.semaphore_signal(ready.at[z], inc=1, device_id=(zs[d] + x, rcv), device_id_type=MESH)
-    plane_start()
-    for dx, dy in PLANE:
-        if dx or dy:
-            scatter(z, dx, dy)
+        pl.semaphore_signal(ready.at[y], inc=1, device_id=(shot, ys[d] * 2 + core), device_id_type=MESH)
+    mask_start(0)
+    for dz, dx in PLANE:
+        if dz or dx:
+            scatter(y, dz, dx)
     pltpu.make_async_copy(spec.at[me], grid.at[core, y, mine], recv1.at[y]).start()
-    for k in range(3):
-        plane = (z + (2, 1, 3)[k]) % 4
-        pl.semaphore_wait(ready.at[plane], 1)
-        for dx, dy in PLANE:
-            scatter(plane, dx, dy)
-    plane_wait()
-    mask_start()
+    for d in (2, 1, 3):
+        pl.semaphore_wait(ready.at[ys[d]], 1)
+        for dz, dx in PLANE:
+            scatter(ys[d], dz, dx)
+    mask_wait(0)
+    mask_start(1)
+    mask_wait(1)
+    mask_start(2)
 
     block = lax.broadcasted_iota(jnp.int32, (128, 1024), 0)
     column = lax.broadcasted_iota(jnp.int32, (128, 1024), 1)
@@ -210,18 +200,18 @@
             device_id_type=MESH,
         )
 
-    for d in (0, 3, 2, 1):
+    for d in (0, 2, 3, 1):
         slab = grid.at[core, ys[d]]
         pltpu.make_async_copy(slab, slab, recv1.at[ys[d]]).wait()
         slab_copy(ys[d]).start()
 
-    mask_wait()
+    mask_wait(2)
     mrow[...] = jnp.dot(
         mtab[...].reshape(CHIPS, 128).astype(jnp.bfloat16), expand, preferred_element_type=jnp.float32
     )
 
     def spread(t, carry):
-        mask[t % NY, t // NY] = jnp.broadcast_to(mrow[pl.ds(t, 1), :], (16, 1024)).astype(jnp.bfloat16)
+        mask[t // NS, t % NS] = jnp.broadcast_to(mrow[pl.ds(t, 1), :], (16, 1024)).astype(jnp.bfloat16)
         return carry
 
     lax.fori_loop(0, CHIPS, spread, 0, unroll=4)
@@ -250,24 +240,22 @@
     for d in BACK:
         ty = ys[d]
         prod[ty] = (acc[d] + half(d, 1)).astype(jnp.bfloat16)
-        for dz, dx in PLANE:
-            if d or dz or dx:
-                ts = zs[dz] + xs[dx]
+        for dz, dx in [(a, b) for a in range(4) for b in (2, 1, 3, 0)]:
+            ts = dz * 4 + xs[dx]
+
+            @pl.when(jnp.logical_or(ts != shot, ty != y))
+            def _():
                 pltpu.make_async_remote_copy(
                     src_ref=prod.at[ty, pl.ds(pl.multiple_of(ts * TS, TS), TS)],
                     dst_ref=back.at[y, shot],
                     send_sem=send2,
-                    recv_sem=recv2.at[d],
+                    recv_sem=recv2,
                     device_id=(ts, ty * 2 + core),
                     device_id_type=MESH,
                 ).start()
-            else:
-                pltpu.make_async_copy(prod.at[y, mine], back.at[y, shot], recv2.at[0]).start()
-
-    for d in BACK:
-        ty = ys[-d % 4]
-        pltpu.make_async_copy(back.at[ty], back.at[ty], recv2.at[d]).wait()
-
+
+    pltpu.make_async_copy(prod.at[y, mine], back.at[y, shot], recv2).start()
+    pltpu.make_async_copy(back, back, recv2).wait()
     for k in range(NY):
         slab_copy(k).wait_send()
     sent = spec.at[pl.ds(0, CHIPS - 1)]
@@ -323,9 +311,9 @@
             dma((NY,)),
             dma((NY,)),
             dma,
-            dma((NY,)),
-            dma((19,)),
-            dma((19,)),
+            dma,
+            dma((9,)),
+            dma((9,)),
             pltpu.SemaphoreType.REGULAR((4,)),
         ],
         compiler_params=pltpu.CompilerParams(

time: 33.2 us -> 32.5 us (0.979)
  Pallas kernels: 33.1 us -> 32.4 us
    pallas_call x1, Pallas kernels: 30.7 us -> 30 us  [local(): pl.pallas_call(kernel, out_shape=jax.ShapeDtypeStruct((NY, NS, TS, 128),...]
where the time goes in v4:
time: 32.5 us; the launch traced here: 32.4 us
  Pallas kernels  32.4 us (100%)
    pallas_call x1, Pallas kernels, local(): pl.pallas_call(kernel, out_shape=jax.ShapeDtypeStruct((NY, NS, TS, 128),...  30 us
    pallas_call x1, Pallas kernels, local(): pl.pallas_call(widen, out_shape=jax.ShapeDtypeStruct((FREQS, 2, TS, TR),...  2.42 us

profile of v4, /device:TPU:0, one launch (start us, length us, event | category | flops | bytes accessed | tf_op | source)
XLA Modules:
  0.0 32.4 jit_solution(17603111837342101733)
XLA Ops:
  0.0 30.0 %multiples.1.back = bf16[4,16,32,128]{3,2,1,0:T(8,128)(2,1)} custom-call(bf16[32,64,1024]{2,1,0:T(8,128)(2,1)} %traces.1, bf16[128,1024]{1,0:T(8,128)(2,1)} %constant.2.clone.table_hbm, s32[1,1,8]{2,1,0:T(1,128)} %lists_hbm.1), custom_call_target="tpu_custom_call" | custom-call | flops 1073741824 | bytes 8388608 | tf_op jit(solution)/shard_map/multiples/pallas_call | solution.py:287
  30.0 2.4 %widen.1 = f32[64,2,32,64]{3,2,1,0:T(8,128)} custom-call(bf16[4,16,32,128]{3,2,1,0:T(8,128)(2,1)} %multiples.1.back), custom_call_target="tpu_custom_call" | custom-call | flops 1048576 | bytes 3145728 | tf_op jit(solution)/shard_map/widen/pallas_call | solution.py:325

commit v5 on v4

--- a/solution.py
+++ b/solution.py
@@ -218,28 +218,36 @@
 
     left64 = lax.broadcasted_iota(jnp.int32, (TR, 128), 1) < TR
 
-    def half(d, h):
+    def part(d, h, slabs):
         par = core if h == 0 else 1 - core
-        for k in range(NY):
-            cols = slice(k * 128, k * 128 + 128)
+        width = len(slabs) * 128
+        for n, ds in enumerate(slabs):
+            k = ys[ds]
             left = grid[par, k].reshape(NS, 2, 16, 128)
-            weights = mask[ys[d], :, :, h * 512 + k * 128 : h * 512 + k * 128 + 128]
-            masked[:, cols] = (left * weights[:, None]).reshape(NS * TS, 128)
+            weights = mask[ys[d], :, :, pl.ds(pl.multiple_of(h * 512 + k * 128, 128), 128)]
+            masked[:, n * 128 : n * 128 + 128] = (left * weights[:, None]).reshape(NS * TS, 128)
             first = pl.multiple_of((2 * k + par) * TR, TR)
-            part = grid[core, ys[d], pl.ds(first, TR), :]
-            turned = pltpu.roll(part.astype(jnp.float32), TR, 1)
-            rhat[k * 128 : k * 128 + TR, :] = part
-            rhat[k * 128 + TR : (k + 1) * 128, :] = jnp.where(left64, -turned, turned).astype(jnp.bfloat16)
-        return jnp.dot(masked[...], rhat[...], preferred_element_type=jnp.float32)
+            right = grid[core, ys[d], pl.ds(first, TR), :]
+            turned = pltpu.roll(right.astype(jnp.float32), TR, 1)
+            rhat[n * 128 : n * 128 + TR, :] = right
+            rhat[n * 128 + TR : (n + 1) * 128, :] = jnp.where(left64, -turned, turned).astype(jnp.bfloat16)
+        return jnp.dot(masked[:, :width], rhat[:width, :], preferred_element_type=jnp.float32)
+
+    def other_slab(ds):
+        slab = grid.at[1 - core, ys[ds]]
+        pltpu.make_async_copy(slab, slab, xrecv.at[ys[ds]]).wait()
 
     for d in range(NY):
-        acc[d] = half(d, 0)
-    for k in range(NY):
-        other = grid.at[1 - core, k]
-        pltpu.make_async_copy(other, other, xrecv.at[k]).wait()
+        acc[d] = part(d, 0, (0, 2, 3, 1))
+    other_slab(0)
+    other_slab(2)
+    for d in range(NY):
+        acc[d] += part(d, 1, (0, 2))
+    other_slab(3)
+    other_slab(1)
     for d in BACK:
         ty = ys[d]
-        prod[ty] = (acc[d] + half(d, 1)).astype(jnp.bfloat16)
+        prod[ty] = (acc[d] + part(d, 1, (3, 1))).astype(jnp.bfloat16)
         for dz, dx in [(a, b) for a in range(4) for b in (2, 1, 3, 0)]:
             ts = dz * 4 + xs[dx]
 

time: 32.5 us -> 32.5 us (level)
  no operation moved by 1% of the time
where the time goes in v5:
time: 32.5 us; the launch traced here: 32.4 us
  Pallas kernels  32.4 us (100%)
    pallas_call x1, Pallas kernels, local(): pl.pallas_call(kernel, out_shape=jax.ShapeDtypeStruct((NY, NS, TS, 128),...  30 us
    pallas_call x1, Pallas kernels, local(): pl.pallas_call(widen, out_shape=jax.ShapeDtypeStruct((FREQS, 2, TS, TR),...  2.42 us

profile of v5, /device:TPU:0, one launch (start us, length us, event | category | flops | bytes accessed | tf_op | source)
XLA Modules:
  0.0 32.4 jit_solution(13789604216895670511)
XLA Ops:
  0.0 30.0 %multiples.1.back = bf16[4,16,32,128]{3,2,1,0:T(8,128)(2,1)} custom-call(bf16[32,64,1024]{2,1,0:T(8,128)(2,1)} %traces.1, bf16[128,1024]{1,0:T(8,128)(2,1)} %constant.2.clone.table_hbm, s32[1,1,8]{2,1,0:T(1,128)} %lists_hbm.1), custom_call_target="tpu_custom_call" | custom-call | flops 1073741824 | bytes 8388608 | tf_op jit(solution)/shard_map/multiples/pallas_call | solution.py:295
  30.0 2.4 %widen.1 = f32[64,2,32,64]{3,2,1,0:T(8,128)} custom-call(bf16[4,16,32,128]{3,2,1,0:T(8,128)(2,1)} %multiples.1.back), custom_call_target="tpu_custom_call" | custom-call | flops 1048576 | bytes 3145728 | tf_op jit(solution)/shard_map/widen/pallas_call | solution.py:333

commit v6 on v4

--- a/solution.py
+++ b/solution.py
@@ -9,7 +9,7 @@
 from jax.experimental.pallas import tpu as pltpu
 from jax.sharding import PartitionSpec as P
 
-MESH = pl.DeviceIdType.MESH
+LOGICAL = pl.DeviceIdType.LOGICAL
 
 NT = 1024
 BAND = 32
@@ -78,7 +78,7 @@
     core = rcv % 2
     z, x = shot // 4, shot % 4
     me = y * NS + shot
-    sibling = (shot, y * 2 + 1 - core)
+    sibling = shot * 8 + y * 2 + 1 - core
     zs = [(z + d) % 4 * 4 for d in range(4)]
     xs = [(x + d) % 4 for d in range(4)]
     ys = [(y + d) % 4 for d in range(4)]
@@ -96,15 +96,15 @@
     lists_load.start()
 
     barrier = pltpu.get_barrier_semaphore()
-    pl.semaphore_signal(barrier, inc=1, device_id=sibling, device_id_type=MESH)
+    pl.semaphore_signal(barrier, inc=1, device_id=sibling, device_id_type=LOGICAL)
     for d in (1, 2, 3):
         pl.semaphore_signal(
-            barrier, inc=1, device_id=(shot, ys[d] * 2 + core), device_id_type=MESH
+            barrier, inc=1, device_id=shot * 8 + ys[d] * 2 + core, device_id_type=LOGICAL
         )
     for dz, dx in PLANE:
         if dz or dx:
             pl.semaphore_signal(
-                barrier, inc=1, device_id=(zs[dz] + xs[dx], rcv), device_id_type=MESH
+                barrier, inc=1, device_id=(zs[dz] + xs[dx]) * 8 + rcv, device_id_type=LOGICAL
             )
 
     lists_load.wait()
@@ -144,8 +144,8 @@
             dst_ref=mtab.at[rows],
             send_sem=msend.at[stage * 3 + d - 1],
             recv_sem=mrecv.at[stage * 3 + d - 1],
-            device_id=to,
-            device_id_type=MESH,
+            device_id=to[0] * 8 + to[1],
+            device_id_type=LOGICAL,
         )
 
     def mask_start(stage):
@@ -165,13 +165,13 @@
             dst_ref=grid.at[core, y, mine],
             send_sem=send1,
             recv_sem=recv1.at[y],
-            device_id=(ts, plane * 2 + core),
-            device_id_type=MESH,
+            device_id=ts * 8 + (plane * 2 + core),
+            device_id_type=LOGICAL,
         ).start()
 
     pl.semaphore_wait(barrier, NS + 3)
     for d in (1, 2, 3):
-        pl.semaphore_signal(ready.at[y], inc=1, device_id=(shot, ys[d] * 2 + core), device_id_type=MESH)
+        pl.semaphore_signal(ready.at[y], inc=1, device_id=shot * 8 + ys[d] * 2 + core, device_id_type=LOGICAL)
     mask_start(0)
     for dz, dx in PLANE:
         if dz or dx:
@@ -197,7 +197,7 @@
             send_sem=xsend.at[ty],
             recv_sem=xrecv.at[ty],
             device_id=sibling,
-            device_id_type=MESH,
+            device_id_type=LOGICAL,
         )
 
     for d in (0, 2, 3, 1):
@@ -242,17 +242,18 @@
         prod[ty] = (acc[d] + half(d, 1)).astype(jnp.bfloat16)
         for dz, dx in [(a, b) for a in range(4) for b in (2, 1, 3, 0)]:
             ts = dz * 4 + xs[dx]
-
-            @pl.when(jnp.logical_or(ts != shot, ty != y))
-            def _():
-                pltpu.make_async_remote_copy(
-                    src_ref=prod.at[ty, pl.ds(pl.multiple_of(ts * TS, TS), TS)],
-                    dst_ref=back.at[y, shot],
-                    send_sem=send2,
-                    recv_sem=recv2,
-                    device_id=(ts, ty * 2 + core),
-                    device_id_type=MESH,
-                ).start()
+            give = pltpu.make_async_remote_copy(
+                src_ref=prod.at[ty, pl.ds(pl.multiple_of(ts * TS, TS), TS)],
+                dst_ref=back.at[y, shot],
+                send_sem=send2,
+                recv_sem=recv2,
+                device_id=ts * 8 + (ty * 2 + core),
+                device_id_type=LOGICAL,
+            )
+            if d:
+                give.start()
+            else:
+                pl.when(ts != shot)(give.start)
 
     pltpu.make_async_copy(prod.at[y, mine], back.at[y, shot], recv2).start()
     pltpu.make_async_copy(back, back, recv2).wait()

time: 32.5 us -> 32.5 us (level)
  no operation moved by 1% of the time
where the time goes in v6:
time: 32.5 us; the launch traced here: 32.4 us
  Pallas kernels  32.4 us (100%)
    pallas_call x1, Pallas kernels, local(): pl.pallas_call(kernel, out_shape=jax.ShapeDtypeStruct((NY, NS, TS, 128),...  30 us
    pallas_call x1, Pallas kernels, local(): pl.pallas_call(widen, out_shape=jax.ShapeDtypeStruct((FREQS, 2, TS, TR),...  2.42 us

profile of v6, /device:TPU:0, one launch (start us, length us, event | category | flops | bytes accessed | tf_op | source)
XLA Modules:
  0.0 32.4 jit_solution(16454868971777117692)
XLA Ops:
  0.0 30.0 %multiples.1.back = bf16[4,16,32,128]{3,2,1,0:T(8,128)(2,1)} custom-call(bf16[32,64,1024]{2,1,0:T(8,128)(2,1)} %traces.1, bf16[128,1024]{1,0:T(8,128)(2,1)} %constant.2.clone.table_hbm, s32[1,1,8]{2,1,0:T(1,128)} %lists_hbm.1), custom_call_target="tpu_custom_call" | custom-call | flops 1073741824 | bytes 8388608 | tf_op jit(solution)/shard_map/multiples/pallas_call | solution.py:288
  30.0 2.4 %widen.1 = f32[64,2,32,64]{3,2,1,0:T(8,128)} custom-call(bf16[4,16,32,128]{3,2,1,0:T(8,128)(2,1)} %multiples.1.back), custom_call_target="tpu_custom_call" | custom-call | flops 1048576 | bytes 3145728 | tf_op jit(solution)/shard_map/widen/pallas_call | solution.py:326

commit v7 on v4

--- a/solution.py
+++ b/solution.py
@@ -27,7 +27,7 @@
 PITCH = 40
 VMEM_MIB = 60
 BACK = (2, 1, 3, 0)
-PLANE = [(a, b) for a in (2, 1, 3, 0) for b in (2, 1, 3, 0)]
+PLANE = [((a + b) % 4, b) for a in (2, 1, 3, 0) for b in (2, 1, 3, 0)]
 
 
 def dft_table():

time: 32.5 us -> 32.5 us (level)
  no operation moved by 1% of the time
where the time goes in v7:
time: 32.5 us; the launch traced here: 32.4 us
  Pallas kernels  32.4 us (100%)
    pallas_call x1, Pallas kernels, local(): pl.pallas_call(kernel, out_shape=jax.ShapeDtypeStruct((NY, NS, TS, 128),...  30 us
    pallas_call x1, Pallas kernels, local(): pl.pallas_call(widen, out_shape=jax.ShapeDtypeStruct((FREQS, 2, TS, TR),...  2.42 us

profile of v7, /device:TPU:0, one launch (start us, length us, event | category | flops | bytes accessed | tf_op | source)
XLA Modules:
  0.0 32.4 jit_solution(17150685556237267199)
XLA Ops:
  0.0 30.0 %multiples.1.back = bf16[4,16,32,128]{3,2,1,0:T(8,128)(2,1)} custom-call(bf16[32,64,1024]{2,1,0:T(8,128)(2,1)} %traces.1, bf16[128,1024]{1,0:T(8,128)(2,1)} %constant.2.clone.table_hbm, s32[1,1,8]{2,1,0:T(1,128)} %lists_hbm.1), custom_call_target="tpu_custom_call" | custom-call | flops 1073741824 | bytes 8388608 | tf_op jit(solution)/shard_map/multiples/pallas_call | solution.py:287
  30.0 2.4 %widen.1 = f32[64,2,32,64]{3,2,1,0:T(8,128)} custom-call(bf16[4,16,32,128]{3,2,1,0:T(8,128)(2,1)} %multiples.1.back), custom_call_target="tpu_custom_call" | custom-call | flops 1048576 | bytes 3145728 | tf_op jit(solution)/shard_map/widen/pallas_call | solution.py:325
